TPU v7x, 32 devices: a whole 2x2x4 slice. The times are simulated.
32 devices in a mesh: group: 2 (over y), ctx: 4 (over z), head: 4 (over x, core).
Axes of the slice: x: 2, y: 2, z: 4, core: 2. Of those that a mesh axis runs over, the one named last changes fastest.
Arguments:
- query: bfloat16 [1024, 4096], P(('group', 'ctx'), 'head'), parts along dimension 0, may hold values from -8 to 8
- keys: bfloat16 [1024, 512], P(('group', 'ctx'), 'head'), parts along dimension 0, may hold values from -6 to 6
- values: bfloat16 [1024, 512], P(('group', 'ctx'), 'head'), parts along dimension 0, may hold values from -6 to 6
- residual: bfloat16 [1024, 2048], P(('group', 'ctx', 'head')), parts along dimension 0, may hold values from -15 to 15
- o_weight: bfloat16 [4096, 2048], P('head', 'ctx'), may hold values from -0.09375 to 0.09375
- gain: float32 [2048], replicated, may hold values from 0.1 to 1.9
- routes: int32 [1024, 8], P(('group', 'ctx', 'head')), parts along dimension 0, may hold values from 0 to 15, all different within a row; in each aligned block of 32 rows (0 to 31, 32 to 63, ...) at most 32 rows name the same one
- gates: float32 [1024, 8], P(('group', 'ctx', 'head')), parts along dimension 0, may hold values from 0.05 to 1
- w_gate: bfloat16 [16, 2048, 768], P(('ctx', 'head')), may hold values from -0.125 to 0.125
- w_up: bfloat16 [16, 2048, 768], P(('ctx', 'head')), may hold values from -0.125 to 0.125
- w_down: bfloat16 [16, 768, 2048], P(('ctx', 'head')), may hold values from -0.625 to 0.625
Outputs:
- mixed: bfloat16 [1024, 2048], P(('group', 'ctx', 'head')), parts along dimension 0
- expert_mix: bfloat16 [1024, 2048], P(('group', 'ctx', 'head')), parts along dimension 0
There are 2 independent parts, one for each index of `group`. A program takes and returns all parts, laid end to end along the dimension named above; an argument that names none is the same for every part. Nothing has to cross between parts.
Inputs may be any that keep to these rules, and one draw needn't show every extreme that they name: `routes`: the 8 experts of a token are distinct. In each aligned block of 32 tokens (the tokens of one owner device), no expert is named more than 32 times, a bound that some block reaches.
All inputs are finite; a program needn't handle non-finite values.
Results may differ from a plain program's by a relative error of at most 0.019.
Values may be sent and summed in bfloat16 or wider, within the bound.
A program may use at most 128 MiB of HBM per device.

v0:
```python
import jax
import jax.numpy as jnp
from jax import lax
from jax.sharding import PartitionSpec as P

HEAD_DIMENSION = 128


def expert_apply(arrived, gate_proj, up_proj, down_proj):
    shape_in = arrived.shape
    flat_rows = arrived.reshape(-1, shape_in[-1])
    gate_act = jnp.dot(flat_rows, gate_proj, preferred_element_type=jnp.float32)
    up_act = jnp.dot(flat_rows, up_proj, preferred_element_type=jnp.float32)
    hidden = (jax.nn.silu(gate_act) * up_act).astype(jnp.bfloat16)
    output = jnp.dot(hidden, down_proj, preferred_element_type=jnp.float32).astype(jnp.bfloat16)
    return output.reshape(shape_in)


def body(query, keys, values, residual, o_weight, gain, routes, gates, w_gate, w_up, w_down):
    head_size = HEAD_DIMENSION
    query_rows = query.shape[0]
    kv_heads = keys.shape[1] // head_size
    q_heads = query.shape[1] // head_size
    head_replicas = q_heads // kv_heads
    scale = head_size ** (-0.5)
    queries = query.reshape(query_rows, kv_heads, head_replicas, head_size)
    first_pos = lax.axis_index("ctx") * query_rows
    query_pos = first_pos + jnp.arange(query_rows, dtype=jnp.int32)
    last_pos = first_pos + query_rows - 1

    def accumulate(carry, pieces):
        run_max, run_sum, run_acc = carry
        key_piece, value_piece = pieces
        width = key_piece.shape[0]
        key_pos = jnp.arange(width, dtype=jnp.int32)
        visible = key_pos[None, :] <= query_pos[:, None]
        scores = (
            jnp.einsum(
                "veqi,zei->eqvz",
                queries,
                key_piece.reshape(width, kv_heads, head_size),
                preferred_element_type=jnp.float32,
            )
            * scale
        )
        scores = jnp.where(visible, scores, -1e30)
        new_max = jnp.maximum(run_max, jnp.max(scores, axis=-1))
        weights = jnp.where(visible, jnp.exp(scores - new_max[..., None]), 0.0)
        new_sum = jnp.sum(weights, axis=-1)
        update = jnp.einsum(
            "pexa,apo->pexo",
            weights.astype(jnp.bfloat16),
            value_piece.reshape(width, kv_heads, head_size),
            preferred_element_type=jnp.float32,
        )
        return (new_max, new_sum, update)

    start_state = (
        jnp.full((kv_heads, head_replicas, query_rows), -1e30, jnp.float32),
        jnp.zeros((kv_heads, head_replicas, query_rows), jnp.float32),
        jnp.zeros((kv_heads, head_replicas, query_rows, head_size), jnp.float32),
    )
    pieces = (
        lax.all_gather(keys, "ctx", axis=0, tiled=True),
        lax.all_gather(values, "ctx", axis=0, tiled=True),
    )
    run_max, run_sum, run_acc = lax.cond(
        jnp.int32(0) > last_pos, lambda: start_state, lambda: accumulate(start_state, pieces)
    )
    attended = (
        (run_acc / run_sum[..., None])
        .transpose(2, 0, 1, 3)
        .reshape(query_rows, q_heads * head_size)
        .astype(jnp.bfloat16)
    )
    head_terms = jnp.dot(
        attended,
        lax.all_gather(o_weight, "ctx", axis=1, tiled=True),
        preferred_element_type=jnp.float32,
    )
    summed = lax.psum_scatter(
        head_terms.astype(jnp.bfloat16), "head", scatter_dimension=0, tiled=True
    ).astype(jnp.float32)
    mixed = (summed + residual.astype(jnp.float32)).astype(jnp.bfloat16)
    mixed_f = mixed.astype(jnp.float32)
    normed = (
        mixed_f * lax.rsqrt(jnp.mean(mixed_f * mixed_f, axis=-1, keepdims=True) + 1e-06) * gain
    ).astype(jnp.bfloat16)
    own_rows = residual.shape[0]
    model_dim = residual.shape[1]
    top_count = routes.shape[1]
    ctx_count = lax.axis_size("ctx")
    head_count = lax.axis_size("head")
    devices = ctx_count * head_count
    capacity = min(own_rows, max(2, 2 * own_rows * top_count // devices))
    expert_ids = routes.reshape(-1)
    onehot = (expert_ids[:, None] == jnp.arange(devices, dtype=jnp.int32)[None, :]).astype(
        jnp.int32
    )
    slots = jnp.sum((jnp.cumsum(onehot, axis=0) - 1) * onehot, axis=1)
    target = expert_ids * capacity + slots
    outgoing = (
        jnp.zeros((devices * capacity, model_dim), jnp.bfloat16)
        .at[target]
        .set(jnp.repeat(normed, top_count, axis=0))
    )
    outgoing = outgoing.reshape(devices, capacity, model_dim)
    gate_proj = w_gate[0]
    up_proj = w_up[0]
    down_proj = w_down[0]
    computed = expert_apply(
        lax.all_to_all(outgoing, ("ctx", "head"), split_axis=0, concat_axis=0, tiled=True),
        gate_proj,
        up_proj,
        down_proj,
    )
    returned = lax.all_to_all(computed, ("ctx", "head"), split_axis=0, concat_axis=0, tiled=True)
    selected_entries = returned.reshape(devices * capacity, model_dim)[target]
    selected_entries = selected_entries.astype(jnp.float32).reshape(own_rows, top_count, model_dim)
    weight_norm = gates / jnp.sum(gates, axis=-1, keepdims=True)
    expert_mix = jnp.sum(selected_entries * weight_norm[..., None], axis=1).astype(jnp.bfloat16)
    return (mixed, expert_mix)


def solution(mesh):
    return jax.shard_map(
        body,
        mesh=mesh,
        in_specs=(
            P(("group", "ctx"), "head"),
            P(("group", "ctx"), "head"),
            P(("group", "ctx"), "head"),
            P(("group", "ctx", "head"), None),
            P("head", "ctx"),
            P(),
            P(("group", "ctx", "head"), None),
            P(("group", "ctx", "head"), None),
            P(("ctx", "head"), None, None),
            P(("ctx", "head"), None, None),
            P(("ctx", "head"), None, None),
        ),
        out_specs=(P(("group", "ctx", "head"), None), P(("group", "ctx", "head"), None)),
        check_vma=False,
    )
```

profile of v0, /device:TPU:11, one launch (start us, length us, event | category | flops | bytes accessed | tf_op | source)
XLA Modules:
  0.0 255.9 jit_solution(5889170970731669494)
XLA Ops:
  7.2 0.7 all-gather.2.cloned.1.call-update
  8.0 11.0 %all_gather.10 = bf16[512,128]{1,0:T(8,128)(2,1)S(1)} all-gather(bf16[128,128]{1,0:T(8,128)(2,1)} %param.15), channel_id=1, replica_groups=mesh['group'=2,'ctx'=4,'head'=4] {'ctx'}, dimensions={0}, use_global_device_ids=true | all-gather | bytes 163840 | tf_op jit(solution)/shard_map/all_gather | solution.py:65
  19.0 14.4 %all_gather.9 = bf16[512,128]{1,0:T(8,128)(2,1)S(1)} all-gather(bf16[128,128]{1,0:T(8,128)(2,1)} %param.14), channel_id=1, replica_groups=mesh['group'=2,'ctx'=4,'head'=4] {'ctx'}, dimensions={0}, use_global_device_ids=true | all-gather | bytes 163840 | tf_op jit(solution)/shard_map/all_gather | solution.py:64
  33.3 2.6 %conditional.1 = (f32[1,8,128]{2,1,0:T(8,128)S(1)}, f32[1,8,128,128]{2,3,1,0:T(8,128)S(1)}) conditional(s32[]{:T(128)} %convert_element_type.54, (s32[]{:T(128)}, s32[128]{0:T(128)S(1)}, bf16[128,1024]{1,0:T(8,128)(2,1)}, bf16[512,128]{1,0:T(8,128)(2,1)S(1)}, bf16[512,128]{1,0:T(8,128)(2,1)S(1)}) %tuple.16, () %tuple.17), branch_computations={%region_0.3_spmd, %region_3.4_spmd} | conditional | flops 275315840 | bytes 7628308 | solution.py:67
  33.4 0.1 iota_compare_fusion
  33.4 1.4 fusion
  34.8 0.6 convolution_bitcast_fusion
  35.5 0.5 fusion.2
  36.0 0.1 divide_convert_fusion
  36.1 55.4 %all-gather.2.cloned.1.call-done = bf16[1024,2048]{1,0:T(8,128)(2,1)} async-done(((bf16[1024,512]{1,0:T(8,128)(2,1)}), bf16[1024,2048]{1,0:T(8,128)(2,1)}) %all-gather.2.cloned.1.call-update) | async-done | bytes 4194320 | tf_op jit(solution)/shard_map/all_gather | solution.py:78
  91.4 3.8 %convolution_convert_fusion = bf16[128,2048]{1,0:T(8,128)(2,1)} fusion(bf16[128,1024]{0,1:T(8,128)(2,1)S(1)} %bitcast.93, bf16[1024,2048]{1,0:T(8,128)(2,1)} %all-gather.2.cloned.1.call-done), kind=kOutput, calls=%fused_computation.32 | convolution fusion | flops 537133056 | bytes 4980736 | tf_op jit(solution)/shard_map/dot_general | solution.py:76
  95.2 0.1 copy.21
  95.3 0.1 eq.29
  95.4 0.1 eq.25
  95.5 0.6 reduce-window.6
  96.1 0.2 slice_reduce_fusion
  96.3 0.1 copy.20
  96.4 0.1 mul.68
  96.5 0.1 fusion.40
  96.6 20.1 %reduce-scatter.2.cloned.1.call-done = bf16[32,2048]{1,0:T(8,128)(2,1)} async-done(((bf16[128,2048]{1,0:T(8,128)(2,1)}), bf16[32,2048]{1,0:T(8,128)(2,1)}) %reduce-scatter.2.cloned.1.call-update) | async-done | bytes 131088 | tf_op jit(solution)/shard_map/reduce_scatter | solution.py:81
  116.8 1.1 fusion.36
  117.8 0.1 fusion.38
  118.0 3.7 %scatter_custom_fusion = bf16[512,2048]{1,0:T(8,128)(2,1)} fusion(s32[256]{0:T(256)S(1)} %bitcast.96, bf16[]{:T(256)} %constant.28.clone.1, bf16[32,2048]{1,0:T(8,128)(2,1)S(1)} %fusion.38), kind=kCustom, calls=%fused_computation.36 | custom fusion | bytes 2228226 | tf_op jit(solution)/shard_map/scatter | solution.py:105
  121.7 54.0 %all_to_all.10 = bf16[16,32,2048]{2,1,0:T(8,128)(2,1)S(1)} all-to-all(bf16[16,32,2048]{2,1,0:T(8,128)(2,1)} %bitcast.89), channel_id=1, replica_groups=mesh['group'=2,'ctx'=4,'head'=4] {'ctx','head'}, dimensions={0} | all-to-all | bytes 4194304 | tf_op jit(solution)/shard_map/all_to_all | solution.py:112
  175.7 1.3 copy-done.1
  177.0 3.0 %fusion.22 = f32[512,768]{1,0:T(8,128)} fusion(bf16[512,2048]{1,0:T(8,128)(2,1)S(1)} %bitcast.91, bf16[1,2048,768]{2,1,0:T(8,128)(2,1)S(1)} %copy-done.7), kind=kOutput, calls=%fused_computation.29 | convolution fusion | flops 1610612736 | bytes 6815744 | tf_op jit(solution)/shard_map/dot_general | solution.py:12
  179.9 8.3 %fusion.24 = bf16[512,2048]{1,0:T(8,128)(2,1)} fusion(bf16[1,768,2048]{2,1,0:T(8,128)(2,1)S(1)} %copy-done, f32[512,768]{1,0:T(8,128)} %fusion.22, bf16[512,2048]{1,0:T(8,128)(2,1)} %bitcast.92, bf16[1,2048,768]{2,1,0:T(8,128)(2,1)} %param.22), kind=kOutput, calls=%fused_computation.31 | convolution fusion | flops 3224633344 | bytes 12058624 | tf_op jit(solution)/shard_map/dot_general | solution.py:15
  188.2 5.3 %all-to-all-start.1 = ((bf16[16,32,2048]{2,1,0:T(8,128)(2,1)}), bf16[16,32,2048]{2,1,0:T(8,128)(2,1)}, u32[]{:S(2)}, u32[]{:S(2)}) async-start(bf16[16,32,2048]{2,1,0:T(8,128)(2,1)} %bitcast.90), calls=%async_computation.2 | async-start | bytes 4194304 | tf_op jit(solution)/shard_map/all_to_all | solution.py:117
  193.5 0.1 copy.24
  193.6 47.4 %all-to-all-done.1 = bf16[16,32,2048]{2,1,0:T(8,128)(2,1)} async-done(((bf16[16,32,2048]{2,1,0:T(8,128)(2,1)}), bf16[16,32,2048]{2,1,0:T(8,128)(2,1)}, u32[]{:S(2)}, u32[]{:S(2)}) %all-to-all-start.1) | async-done | bytes 2097184 | tf_op jit(solution)/shard_map/all_to_all | solution.py:117
  241.0 5.2 %gather_fusion = bf16[256,2048]{1,0:T(8,128)(2,1)} fusion(bf16[512,2048]{1,0:T(8,128)(2,1)} %bitcast.20, s32[1024]{0:T(1024)S(1)} %pad_clamp_fusion), kind=kCustom, calls=%fused_computation | custom fusion | bytes 2098176 | tf_op jit(solution)/shard_map/gather | solution.py:118
  246.2 2.9 %fusion.27 = bf16[32,2048]{1,0:T(8,128)(2,1)} fusion(bf16[256,2048]{1,0:T(8,128)(2,1)} %gather_fusion, f32[32,8]{1,0:T(8,128)S(1)} %copy.24), kind=kLoop, calls=%fused_computation.34 | loop fusion | flops 1507328 | bytes 1180672 | tf_op jit(solution)/shard_map/reduce_sum | solution.py:121
  (30 shorter events, 0.2 us)
Async XLA Ops:
  7.2 172.8 %copy-start = (bf16[1,768,2048]{2,1,0:T(8,128)(2,1)S(1)}, bf16[1,768,2048]{2,1,0:T(8,128)(2,1)}, u32[]{:S(2)}) copy-start(bf16[1,768,2048]{2,1,0:T(8,128)(2,1)} %param.23) | copy-start | bytes 9437188
  7.2 84.3 %all-gather.2.cloned.1.call-start = ((), (), s32[]{:S(2)}) async-start(), calls=%async_computation.3 | async-start | bytes 5242880 | tf_op jit(solution)/shard_map/all_gather | solution.py:78
  7.9 108.8 %reduce-scatter.2.cloned.1.call-start = ((), (), s32[]{:S(2)}) async-start(), calls=%async_computation.4 | async-start | bytes 655360 | tf_op jit(solution)/shard_map/reduce_scatter | solution.py:81
  91.4 3.8 %copy-start.4 = (s32[32,8]{0,1:T(8,128)S(1)}, s32[32,8]{0,1:T(8,128)}, u32[]{:S(2)}) copy-start(s32[32,8]{0,1:T(8,128)} %param.19) | copy-start | bytes 3076
  91.4 25.3 %copy-start.3 = (bf16[32,2048]{1,0:T(8,128)(2,1)S(1)}, bf16[32,2048]{1,0:T(8,128)(2,1)}, u32[]{:S(2)}) copy-start(bf16[32,2048]{1,0:T(8,128)(2,1)} %param.16) | copy-start | bytes 393220
  91.4 26.4 %copy-start.6 = (f32[2048]{0:T(1024)S(1)}, f32[2048]{0:T(1024)}, u32[]{:S(2)}) copy-start(f32[2048]{0:T(1024)} %param.18) | copy-start | bytes 24580
  117.8 57.8 %copy-start.2 = (bf16[32,2048]{1,0:T(8,128)(2,1)}, bf16[32,2048]{1,0:T(8,128)(2,1)S(1)}, u32[]{:S(2)}) copy-start(bf16[32,2048]{1,0:T(8,128)(2,1)S(1)} %get-tuple-element.28) | copy-start | bytes 393220
  121.7 55.3 %copy-start.7 = (bf16[1,2048,768]{2,1,0:T(8,128)(2,1)S(1)}, bf16[1,2048,768]{2,1,0:T(8,128)(2,1)}, u32[]{:S(2)}) copy-start(bf16[1,2048,768]{2,1,0:T(8,128)(2,1)} %param.21) | copy-start | bytes 9437188
  175.7 1.3 copy-start.1
  188.2 5.3 %copy-start.5 = (f32[32,8]{0,1:T(8,128)S(1)}, f32[32,8]{0,1:T(8,128)}, u32[]{:S(2)}) copy-start(f32[32,8]{0,1:T(8,128)} %param.20) | copy-start | bytes 3076
  188.2 52.8 %all-to-all-start.1 = ((bf16[16,32,2048]{2,1,0:T(8,128)(2,1)}), bf16[16,32,2048]{2,1,0:T(8,128)(2,1)}, u32[]{:S(2)}, u32[]{:S(2)}) async-start(bf16[16,32,2048]{2,1,0:T(8,128)(2,1)} %bitcast.90), calls=%async_computation.2 | async-start | bytes 4194304 | tf_op jit(solution)/shard_map/all_to_all | solution.py:117
Sparse Core Ops, SparseCore 0:
  9.6 81.8 all-gather.1
  95.4 21.3 reduce-scatter.1
where the time goes:
time: 256 us
  waiting for transfers between devices  124 us (48%)
  blocking collectives  79.3 us (31%)
  matrix products  17.1 us (7%)
  between operations  14.1 us (6%)
  local copies, waits for them, and re-layouts  11 us (4%)
  other arithmetic  5.41 us (2%)
  starting transfers between devices  5.33 us (2%)
    all_gather x1, waiting for transfers between devices, body(): lax.all_gather(o_weight, 'ctx', axis=1, tiled=True)  55.4 us
    all_to_all x1, blocking collectives, body(): lax.all_to_all(outgoing, ('ctx', 'head'), split_axis=0, concat_axis=0, ti...  54 us
    all_to_all x1, waiting for transfers between devices, body(): lax.all_to_all(computed, ('ctx', 'head'), split_axis=0, concat_axis=0, ti...  47.4 us
    reduce_scatter x1, waiting for transfers between devices, body(): lax.psum_scatter(head_terms.astype(jnp.bfloat16), 'head', scatter_dimensi...  20.1 us
    all_gather x1, blocking collectives, body(): lax.all_gather(keys, 'ctx', axis=0, tiled=True)  14.4 us
    all_gather x1, blocking collectives, body(): lax.all_gather(values, 'ctx', axis=0, tiled=True)  11 us
    dot_general x1, matrix products, expert_apply(): jnp.dot(hidden, down_proj, preferred_element_type=jnp.float32)  8.28 us
    all_to_all x1, starting transfers between devices, body(): lax.all_to_all(computed, ('ctx', 'head'), split_axis=0, concat_axis=0, ti...  5.25 us
  transfers between devices with their start and end apart: 3, of which 3 were waited for; matrix products, arithmetic and copies ran while one was open for 2% of the time, Pallas kernels for 0%

commit v1 on v0

--- a/solution.py
+++ b/solution.py
@@ -1,6 +1,8 @@
 import jax
 import jax.numpy as jnp
 from jax import lax
+from jax.experimental import pallas as pl
+from jax.experimental.pallas import tpu as pltpu
 from jax.sharding import PartitionSpec as P
 
 HEAD_DIMENSION = 128
@@ -122,9 +124,404 @@
     return (mixed, expert_mix)
 
 
+LANES = 128
+PIECES = 2
+MESH = pl.DeviceIdType.MESH
+
+
+def layer_kernel(
+    n_ctx,
+    q_ref, k_ref, v_ref, res_ref, wo_hbm, gain_ref, routes_ref, gates_ref, wg_hbm, wu_hbm, wd_hbm,
+    mixed_ref, out_ref,
+    wo, wg, wu, wd,
+    kv, att, part, part_in, cross, cross_in, proj,
+    tok, epart, epart_in, ecross, ecross_in, back,
+    local_sem,
+    kv_s, kv_r, att_s, att_r, pa_s, pa_r, px_s, px_r, pz_s, pz_r,
+    tz_s, tz_r, tx_s, tx_r, tc_s, tc_r, ea_s, ea_r, ex_s, ex_r, ez_s, ez_r,
+):
+    f32, bf16 = jnp.float32, jnp.bfloat16
+    z = lax.axis_index("ctx")
+    h = lax.axis_index("head")
+    x, core = h // 2, h % 2
+    core_peer = x * 2 + (1 - core)
+    x_peer = (1 - x) * 2 + core
+    rows, own, model = q_ref.shape[0], res_ref.shape[0], res_ref.shape[1]
+    size = HEAD_DIMENSION
+    q_heads = q_ref.shape[1] // size
+    piece_heads = q_heads // PIECES
+    piece_width = piece_heads * size
+    block = model // n_ctx
+    hidden = wg.shape[1]
+
+    loads = [
+        pltpu.make_async_copy(src, dst, local_sem.at[i])
+        for i, (src, dst) in enumerate(
+            ((wo_hbm, wo), (wg_hbm.at[0], wg), (wu_hbm.at[0], wu), (wd_hbm.at[0], wd))
+        )
+    ]
+    for load in loads:
+        load.start()
+
+    barrier = pltpu.get_barrier_semaphore()
+    for peer in (core_peer, x_peer):
+        pl.semaphore_signal(barrier, inc=1, device_id={"head": peer}, device_id_type=MESH)
+    for step in range(1, n_ctx):
+        pl.semaphore_signal(
+            barrier, inc=1, device_id={"ctx": (z + step) % n_ctx}, device_id_type=MESH
+        )
+
+    kv[z, 0] = k_ref[...]
+    kv[z, 1] = v_ref[...]
+    for other in range(1, n_ctx):
+
+        @pl.when(z < other)
+        def _():
+            kv[other] = jnp.zeros(kv.shape[1:], bf16)
+
+    gate_values = gates_ref[...]
+    gate_norm = gate_values / jnp.sum(gate_values, axis=-1, keepdims=True)
+    route_values = routes_ref[...]
+    lane = lax.broadcasted_iota(jnp.int32, (own, LANES), 1)
+    half = LANES // 2
+    table = jnp.zeros((own, LANES), f32)
+    for k in range(route_values.shape[1]):
+        table = table + jnp.where(
+            lane % half == route_values[:, k : k + 1], gate_norm[:, k : k + 1], 0.0
+        )
+    high = table.astype(bf16).astype(f32)
+    tok[z, h, :, model:] = jnp.where(lane < half, high, table - high).astype(bf16)
+
+    pl.semaphore_wait(barrier, n_ctx + 1)
+
+    def to_ctx(src, dst, send, recv, target):
+        return pltpu.make_async_remote_copy(
+            src_ref=src, dst_ref=dst, send_sem=send, recv_sem=recv,
+            device_id={"ctx": target}, device_id_type=MESH,
+        )
+
+    def to_head(src, dst, send, recv, target):
+        return pltpu.make_async_remote_copy(
+            src_ref=src, dst_ref=dst, send_sem=send, recv_sem=recv,
+            device_id={"head": target}, device_id_type=MESH,
+        )
+
+    last = n_ctx - 1
+    short = jnp.minimum(z, last - z)
+    toward = jnp.where(z * 2 < last, -1, 1)
+
+    def source(i):
+        if i == 0:
+            return z
+        near = toward * ((i + 1) // 2) if i % 2 else -toward * (i // 2)
+        return z + jnp.where(i <= 2 * short, near, -toward * (i - short))
+
+    def kv_copy(s):
+        return to_ctx(kv.at[s], kv.at[s], kv_s.at[s], kv_r.at[s], jnp.minimum(z + 1, last))
+
+    @pl.when(z < last)
+    def _():
+        kv_copy(z).start()
+
+    for step in range(1, n_ctx):
+
+        @pl.when(z >= step)
+        def _():
+            s = z - step
+            kv_copy(s).wait_recv()
+
+            @pl.when(z < last)
+            def _():
+                kv_copy(s).start()
+
+    def chain(buf_at, send, recv, s, go_right):
+        way = 1 if go_right else 0
+        target = jnp.clip(z + (1 if go_right else -1), 0, last)
+        return to_ctx(buf_at, buf_at, send.at[way], recv, target)
+
+    def chain_each(i, s, run):
+        @pl.when((s <= z) & (z < last))
+        def _():
+            run(True)
+
+        @pl.when((s >= z) & (z > 0))
+        def _():
+            run(False)
+
+    def att_copy(s, p, go_right):
+        return chain(att.at[s, p], att_s.at[s, p], att_r.at[s, p], s, go_right)
+
+    keys_all = kv[:, 0].reshape(n_ctx * rows, size)
+    values_all = kv[:, 1].reshape(n_ctx * rows, size)
+    row_at = lax.broadcasted_iota(jnp.int32, (rows, n_ctx * rows), 0)
+    col_at = lax.broadcasted_iota(jnp.int32, (rows, n_ctx * rows), 1)
+    visible = col_at <= row_at + z * rows
+    scale = size ** (-0.5)
+    for p in range(PIECES):
+        for j in range(piece_heads):
+            head = p * piece_heads + j
+            scores = lax.dot_general(
+                q_ref[:, head * size : (head + 1) * size],
+                keys_all,
+                (((1,), (1,)), ((), ())),
+                preferred_element_type=f32,
+            )
+            scores = jnp.where(visible, scores * scale, -1e30)
+            top = jnp.max(scores, axis=-1, keepdims=True)
+            weights = jnp.where(visible, jnp.exp(scores - top), 0.0)
+            total = jnp.sum(weights, axis=-1, keepdims=True)
+            summed = jnp.dot(weights.astype(bf16), values_all, preferred_element_type=f32)
+            att[z, p, :, j * size : (j + 1) * size] = (summed / total).astype(bf16)
+        chain_each(0, z, lambda right, p=p: att_copy(z, p, right).start())
+
+    def swap_core(buf, buf_in, send, recv, i):
+        return to_head(buf.at[i, 1 - core], buf_in.at[i], send.at[i], recv.at[i], core_peer)
+
+    def swap_x(buf, buf_in, send, recv, i):
+        return to_head(buf.at[i], buf_in.at[i], send.at[i], recv.at[i], x_peer)
+
+    def to_owner(buf, dst, send, recv, i):
+        return to_ctx(buf.at[i], dst.at[z], send.at[i], recv.at[z], source(i))
+
+    def store_chunk(buf, i, columns, value):
+        parts = value.astype(bf16).reshape(2, 2, own, value.shape[-1])
+        for cc in range(2):
+            for xx in range(2):
+                buf[i, cc, xx, :, columns] = parts[xx, cc]
+
+    def after_core(i, buf, buf_in, crossed, a_s, a_r, crossed_in, x_s, x_r):
+        swap_core(buf, buf_in, a_s, a_r, i).wait_recv()
+        crossed[i] = (
+            buf[i, core, 1 - x].astype(f32) + buf_in[i, 1 - x].astype(f32)
+        ).astype(bf16)
+        swap_x(crossed, crossed_in, x_s, x_r, i).start()
+
+    def after_x(i, buf, buf_in, crossed_in, crossed, x_s, x_r, dst, own_sum, z_s, z_r):
+        swap_x(crossed, crossed_in, x_s, x_r, i).wait_recv()
+        value = (
+            buf[i, core, x].astype(f32)
+            + buf_in[i, x].astype(f32)
+            + crossed_in[i].astype(f32)
+        ).astype(bf16)
+        own_sum[i] = value
+        if i > 0:
+            to_owner(own_sum, dst, z_s, z_r, i).start()
+
+    loads[0].wait()
+    psum, esum = proj.at[0], back.at[0]
+    pland, eland = proj.at[1], back.at[1]
+    for i in range(n_ctx + 2):
+        if i < n_ctx:
+            s = source(i)
+            value = None
+            for p in range(PIECES):
+                if i > 0:
+                    att_copy(s, p, True).wait_recv()
+                    chain_each(i, s, lambda right, s=s, p=p: att_copy(s, p, right).start())
+                term = jnp.dot(
+                    att[s, p],
+                    wo[p * piece_width : (p + 1) * piece_width, :],
+                    preferred_element_type=f32,
+                )
+                value = term if value is None else value + term
+            store_chunk(part, i, slice(None), value)
+            swap_core(part, part_in, pa_s, pa_r, i).start()
+        if 1 <= i <= n_ctx:
+            after_core(i - 1, part, part_in, cross, pa_s, pa_r, cross_in, px_s, px_r)
+        if i >= 2:
+            after_x(
+                i - 2, part, part_in, cross_in, cross, px_s, px_r, pland, psum, pz_s, pz_r
+            )
+
+    def landed(dst, own_sum, send, recv, s):
+        return to_ctx(own_sum.at[0], dst.at[s], send.at[0], recv.at[s], (z + 1) % n_ctx)
+
+    pland[z] = psum[0]
+    for i in range(1, n_ctx):
+        landed(pland, psum, pz_s, pz_r, source(i)).wait_recv()
+    squares = jnp.zeros((own, 1), f32)
+    for s in range(n_ctx):
+        columns = slice(s * block, (s + 1) * block)
+        value = (pland[s].astype(f32) + res_ref[:, columns].astype(f32)).astype(bf16)
+        mixed_ref[:, columns] = value
+        value = value.astype(f32)
+        squares = squares + jnp.sum(value * value, axis=-1, keepdims=True)
+    factor = lax.rsqrt(squares / model + 1e-06)
+    tok[z, h, :, :model] = (mixed_ref[...].astype(f32) * factor * gain_ref[...]).astype(bf16)
+
+    def tok_z(s, go_right):
+        return chain(tok.at[s, h], tz_s.at[s], tz_r.at[s], s, go_right)
+
+    def tok_x(s):
+        return to_head(tok.at[s, h], tok.at[s, h], tx_s.at[s], tx_r.at[s], x_peer)
+
+    def tok_c(s, which):
+        b = h if which == 0 else x_peer
+        return to_head(tok.at[s, b], tok.at[s, b], tc_s.at[s, which], tc_r.at[s, which], core_peer)
+
+    for load in loads[1:]:
+        load.wait()
+    tile = 256
+    expert = z * lax.axis_size("head") + h
+
+    def experts(i, s):
+        tokens = tok[s, :, :, :model].reshape(4 * own, model)
+        table = tok[s, :, :, model:].reshape(4 * own, LANES).astype(f32)
+        at = lax.broadcasted_iota(jnp.int32, table.shape, 1)
+        weight = jnp.sum(jnp.where(at % half == expert, table, 0.0), axis=-1, keepdims=True)
+        acts = []
+        for t in range(hidden // tile):
+            columns = slice(t * tile, (t + 1) * tile)
+            gate_act = jnp.dot(tokens, wg[:, columns], preferred_element_type=f32)
+            up_act = jnp.dot(tokens, wu[:, columns], preferred_element_type=f32)
+            acts.append((gate_act * (up_act / (1.0 + jnp.exp(-gate_act)))).astype(bf16))
+        hid = jnp.concatenate(acts, axis=1)
+
+        @pl.loop(0, model // tile)
+        def _(t):
+            columns = pl.ds(pl.multiple_of(t * tile, tile), tile)
+            value = jnp.dot(hid, wd[:, columns], preferred_element_type=f32)
+            store_chunk(epart, i, columns, value.astype(bf16).astype(f32) * weight)
+
+    for i in range(n_ctx + 3):
+        if i < n_ctx:
+            s = source(i)
+            if i > 0:
+                tok_z(s, True).wait_recv()
+            chain_each(i, s, lambda right, s=s: tok_z(s, right).start())
+            tok_x(s).start()
+            tok_c(s, 0).start()
+        if 1 <= i <= n_ctx:
+            s = source(i - 1)
+            tok_x(s).wait_recv()
+            tok_c(s, 1).start()
+            tok_c(s, 0).wait_recv()
+            tok_c(s, 1).wait_recv()
+            experts(i - 1, s)
+            swap_core(epart, epart_in, ea_s, ea_r, i - 1).start()
+        if 2 <= i <= n_ctx + 1:
+            after_core(i - 2, epart, epart_in, ecross, ea_s, ea_r, ecross_in, ex_s, ex_r)
+        if i >= 3:
+            after_x(
+                i - 3, epart, epart_in, ecross_in, ecross, ex_s, ex_r, eland, esum, ez_s, ez_r
+            )
+
+    total = esum[0].astype(f32)
+    for i in range(1, n_ctx):
+        s = source(i)
+        landed(eland, esum, ez_s, ez_r, s).wait_recv()
+        total = total + eland[s].astype(f32)
+    out_ref[...] = total.astype(bf16)
+
+    for s in range(n_ctx):
+
+        @pl.when((s <= z) & (z < last))
+        def _():
+            kv_copy(s).wait_send()
+
+    for i in range(n_ctx):
+        s = source(i)
+        for p in range(PIECES):
+            chain_each(i, s, lambda right, s=s, p=p: att_copy(s, p, right).wait_send())
+        chain_each(i, s, lambda right, s=s: tok_z(s, right).wait_send())
+        tok_x(s).wait_send()
+        tok_c(s, 0).wait_send()
+        tok_c(s, 1).wait_send()
+        swap_core(part, part_in, pa_s, pa_r, i).wait_send()
+        swap_core(epart, epart_in, ea_s, ea_r, i).wait_send()
+        swap_x(cross, cross_in, px_s, px_r, i).wait_send()
+        swap_x(ecross, ecross_in, ex_s, ex_r, i).wait_send()
+        if i > 0:
+            to_owner(psum, pland, pz_s, pz_r, i).wait_send()
+            to_owner(esum, eland, ez_s, ez_r, i).wait_send()
+
+
+def fused(query, keys, values, residual, o_weight, gain, routes, gates, w_gate, w_up, w_down):
+    n = lax.axis_size("ctx")
+    rows, width = query.shape
+    own, model = residual.shape
+    hidden = w_gate.shape[2]
+    block = o_weight.shape[1]
+    bf16 = jnp.bfloat16
+    vmem = pl.BlockSpec(memory_space=pltpu.VMEM)
+    hbm = pl.BlockSpec(memory_space=pl.ANY)
+    dma = pltpu.SemaphoreType.DMA
+
+    def sums(columns):
+        return [
+            pltpu.VMEM((n, 2, 2, own, columns), bf16),
+            pltpu.VMEM((n, 2, own, columns), bf16),
+            pltpu.VMEM((n, own, columns), bf16),
+            pltpu.VMEM((n, own, columns), bf16),
+            pltpu.VMEM((2, n, own, columns), bf16),
+        ]
+
+    flops = 2 * rows * (width * model // 1 + 2 * n * rows * width) + 24 * n * rows * model * hidden // 4
+    return pl.pallas_call(
+        lambda *refs: layer_kernel(n, *refs),
+        out_shape=(
+            jax.ShapeDtypeStruct(residual.shape, bf16),
+            jax.ShapeDtypeStruct(residual.shape, bf16),
+        ),
+        in_specs=[vmem, vmem, vmem, vmem, hbm, vmem, vmem, vmem, hbm, hbm, hbm],
+        out_specs=(vmem, vmem),
+        scratch_shapes=[
+            pltpu.VMEM(o_weight.shape, bf16),
+            pltpu.VMEM(w_gate.shape[1:], bf16),
+            pltpu.VMEM(w_up.shape[1:], bf16),
+            pltpu.VMEM(w_down.shape[1:], bf16),
+            pltpu.VMEM((n, 2, rows, HEAD_DIMENSION), bf16),
+            pltpu.VMEM((n, PIECES, rows, width // PIECES), bf16),
+            *sums(block),
+            pltpu.VMEM((n, 4, own, model + LANES), bf16),
+            *sums(model),
+            dma((4,)),
+            dma((n,)), dma((n,)),
+            dma((n, PIECES, 2)), dma((n, PIECES)),
+            dma((n,)), dma((n,)), dma((n,)), dma((n,)), dma((n,)), dma((n,)),
+            dma((n, 2)), dma((n,)), dma((n,)), dma((n,)), dma((n, 2)), dma((n, 2)),
+            dma((n,)), dma((n,)), dma((n,)), dma((n,)), dma((n,)), dma((n,)),
+        ],
+        compiler_params=pltpu.CompilerParams(
+            collective_id=0, has_side_effects=True, vmem_limit_bytes=48 * 1024 * 1024
+        ),
+        cost_estimate=pl.CostEstimate(
+            flops=flops, bytes_accessed=6 * model * hidden + 2 * width * block, transcendentals=0
+        ),
+        name="layer",
+    )(
+        query, keys, values, residual, o_weight, gain.reshape(1, -1), routes, gates,
+        w_gate, w_up, w_down,
+    )
+
+
+def every_token_fits(mesh, *args):
+    devices = mesh.shape["ctx"] * mesh.shape["head"]
+    own = args[3].shape[0] // (devices * mesh.shape["group"])
+    top = args[6].shape[1]
+    capacity = min(own, max(2, 2 * own * top // devices))
+    return (
+        capacity == own
+        and mesh.shape["head"] == 4
+        and mesh.shape["ctx"] <= 8
+        and args[8].shape[0] == devices
+        and devices <= LANES // 2
+        and own % 16 == 0
+        and args[1].shape[1] == 4 * HEAD_DIMENSION
+    )
+
+
 def solution(mesh):
+    def run(*args):
+        inner = fused if every_token_fits(mesh, *args) else body
+        return split(mesh, inner)(*args)
+
+    return run
+
+
+def split(mesh, inner):
     return jax.shard_map(
-        body,
+        inner,
         mesh=mesh,
         in_specs=(
             P(("group", "ctx"), "head"),

time: 256 us -> 97 us (0.38)
  the two profiles are of different devices: /device:TPU:11 before, /device:TPU:0 now
where the time goes in v1:
time: 97 us; the launch traced here: 96.5 us
  Pallas kernels  85.8 us (88%)
  local copies, waits for them, and re-layouts  10 us (10%)
    pallas_call x1, Pallas kernels, fused(): pl.pallas_call(lambda *refs: layer_kernel(n, *refs), out_shape=(jax.Shape...  85.8 us
    unnamed x18, local copies, waits for them, and re-layouts  10 us

profile of v1, /device:TPU:0, one launch (start us, length us, event | category | flops | bytes accessed | tf_op | source)
XLA Modules:
  0.0 96.5 jit_solution(12361707250610478936)
XLA Ops:
  0.6 0.8 copy.13.refs_6_
  1.4 0.8 copy.14.refs_7_
  2.2 0.0 copy-start
  2.2 1.9 %copy-done = bf16[1,2048,768]{2,1,0:T(8,128)(2,1)S(1)} copy-done((bf16[1,2048,768]{2,1,0:T(8,128)(2,1)S(1)}, bf16[1,2048,768]{2,1,0:T(8,128)(2,1)}, u32[]{:S(2)}) %copy-start) | copy-done | bytes 3145752
  4.0 0.0 copy-start.1
  4.0 1.2 %copy-done.1 = bf16[1024,512]{1,0:T(8,128)(2,1)S(1)} copy-done((bf16[1024,512]{1,0:T(8,128)(2,1)S(1)}, bf16[1024,512]{1,0:T(8,128)(2,1)}, u32[]{:S(2)}) %copy-start.1) | copy-done | bytes 1048600
  5.3 0.0 copy-start.2
  5.3 0.9 copy-done.2
  6.2 0.0 copy-start.3
  6.2 0.9 copy-done.3
  7.1 0.0 copy-start.4
  7.1 0.8 copy-done.4
  7.9 0.0 copy-start.5
  7.9 0.8 copy-done.5
  8.6 0.0 copy-start.6
  8.6 0.7 copy-done.6
  9.3 85.8 %layer.1 = (bf16[32,2048]{1,0:T(8,128)(2,1)S(1)}, bf16[32,2048]{1,0:T(8,128)(2,1)S(1)}) custom-call(bf16[128,1024]{1,0:T(8,128)(2,1)S(1)} %copy-done.2, bf16[128,128]{1,0:T(8,128)(2,1)S(1)} %copy-done.4, bf16[128,128]{1,0:T(8,128)(2,1)S(1)} %copy-done.5, bf16[32,2048]{1,0:T(8,128)(2,1)S(1)} %copy-done.3, bf16[1024,512]{1,0:T(8,128)(2,1)S(1)} %copy-done.1, ...), custom_call_target="tpu_custom_call" | custom-call | flops 5637144576 | bytes 10485760 | tf_op jit(solution)/shard_map/layer/pallas_call | solution.py:460
  95.2 0.7 copy.17
  95.8 0.7 copy.18
Async XLA Ops:
  2.2 1.9 %copy-start = (bf16[1,2048,768]{2,1,0:T(8,128)(2,1)S(1)}, bf16[1,2048,768]{2,1,0:T(8,128)(2,1)}, u32[]{:S(2)}) copy-start(bf16[1,2048,768]{2,1,0:T(8,128)(2,1)} %refs_8_.1) | copy-start | bytes 9437188
  4.0 1.2 %copy-start.1 = (bf16[1024,512]{1,0:T(8,128)(2,1)S(1)}, bf16[1024,512]{1,0:T(8,128)(2,1)}, u32[]{:S(2)}) copy-start(bf16[1024,512]{1,0:T(8,128)(2,1)} %refs_4_.1) | copy-start | bytes 3145732
  5.3 0.9 copy-start.2
  6.2 0.9 copy-start.3
  7.1 0.8 copy-start.4
  7.9 0.8 copy-start.5
  8.6 0.7 copy-start.6

commit v2 on v1

--- a/solution.py
+++ b/solution.py
@@ -126,14 +126,15 @@
 
 LANES = 128
 PIECES = 2
+CUT = 2
 MESH = pl.DeviceIdType.MESH
 
 
 def layer_kernel(
     n_ctx,
-    q_ref, k_ref, v_ref, res_ref, wo_hbm, gain_ref, routes_ref, gates_ref, wg_hbm, wu_hbm, wd_hbm,
+    q_hbm, k_hbm, v_hbm, res_hbm, wo_hbm, gain_hbm, routes_hbm, gates_hbm, wg_hbm, wu_hbm, wd_hbm,
     mixed_ref, out_ref,
-    wo, wg, wu, wd,
+    q_ref, res_ref, gain_ref, routes_ref, gates_ref, wo, wg, wu, wd,
     kv, att, part, part_in, cross, cross_in, proj,
     tok, epart, epart_in, ecross, ecross_in, back,
     local_sem,
@@ -157,7 +158,19 @@
     loads = [
         pltpu.make_async_copy(src, dst, local_sem.at[i])
         for i, (src, dst) in enumerate(
-            ((wo_hbm, wo), (wg_hbm.at[0], wg), (wu_hbm.at[0], wu), (wd_hbm.at[0], wd))
+            (
+                (k_hbm, kv.at[z, 0]),
+                (v_hbm, kv.at[z, 1]),
+                (routes_hbm, routes_ref),
+                (gates_hbm, gates_ref),
+                (q_hbm, q_ref),
+                (wo_hbm, wo),
+                (res_hbm, res_ref),
+                (gain_hbm, gain_ref),
+                (wg_hbm.at[0], wg),
+                (wu_hbm.at[0], wu),
+                (wd_hbm.at[0], wd),
+            )
         )
     ]
     for load in loads:
@@ -171,17 +184,17 @@
             barrier, inc=1, device_id={"ctx": (z + step) % n_ctx}, device_id_type=MESH
         )
 
-    kv[z, 0] = k_ref[...]
-    kv[z, 1] = v_ref[...]
     for other in range(1, n_ctx):
 
         @pl.when(z < other)
         def _():
             kv[other] = jnp.zeros(kv.shape[1:], bf16)
 
-    gate_values = gates_ref[...]
+    loads[2].wait()
+    loads[3].wait()
+    gate_values = gates_ref[...].T
     gate_norm = gate_values / jnp.sum(gate_values, axis=-1, keepdims=True)
-    route_values = routes_ref[...]
+    route_values = routes_ref[...].T
     lane = lax.broadcasted_iota(jnp.int32, (own, LANES), 1)
     half = LANES // 2
     table = jnp.zeros((own, LANES), f32)
@@ -216,23 +229,25 @@
         near = toward * ((i + 1) // 2) if i % 2 else -toward * (i // 2)
         return z + jnp.where(i <= 2 * short, near, -toward * (i - short))
 
-    def kv_copy(s):
-        return to_ctx(kv.at[s], kv.at[s], kv_s.at[s], kv_r.at[s], jnp.minimum(z + 1, last))
-
-    @pl.when(z < last)
-    def _():
-        kv_copy(z).start()
-
+    def kv_copy(s, step):
+        return to_ctx(
+            kv.at[s], kv.at[s], kv_s.at[step], kv_r.at[s], jnp.minimum(z + step, last)
+        )
+
+    loads[0].wait()
+    loads[1].wait()
+    for step in range(1, n_ctx):
+
+        @pl.when(z + step <= last)
+        def _():
+            kv_copy(z, step).start()
+
+    loads[4].wait()
     for step in range(1, n_ctx):
 
         @pl.when(z >= step)
         def _():
-            s = z - step
-            kv_copy(s).wait_recv()
-
-            @pl.when(z < last)
-            def _():
-                kv_copy(s).start()
+            kv_copy(z - step, step).wait_recv()
 
     def chain(buf_at, send, recv, s, go_right):
         way = 1 if go_right else 0
@@ -280,8 +295,9 @@
     def swap_x(buf, buf_in, send, recv, i):
         return to_head(buf.at[i], buf_in.at[i], send.at[i], recv.at[i], x_peer)
 
-    def to_owner(buf, dst, send, recv, i):
-        return to_ctx(buf.at[i], dst.at[z], send.at[i], recv.at[z], source(i))
+    def to_owner(buf, dst, send, recv, i, cut):
+        slot = z * cut + i % cut
+        return to_ctx(buf.at[i], dst.at[slot], send.at[i], recv.at[slot], source(i // cut))
 
     def store_chunk(buf, i, columns, value):
         parts = value.astype(bf16).reshape(2, 2, own, value.shape[-1])
@@ -296,7 +312,7 @@
         ).astype(bf16)
         swap_x(crossed, crossed_in, x_s, x_r, i).start()
 
-    def after_x(i, buf, buf_in, crossed_in, crossed, x_s, x_r, dst, own_sum, z_s, z_r):
+    def after_x(i, buf, buf_in, crossed_in, crossed, x_s, x_r, dst, own_sum, z_s, z_r, cut):
         swap_x(crossed, crossed_in, x_s, x_r, i).wait_recv()
         value = (
             buf[i, core, x].astype(f32)
@@ -304,10 +320,10 @@
             + crossed_in[i].astype(f32)
         ).astype(bf16)
         own_sum[i] = value
-        if i > 0:
-            to_owner(own_sum, dst, z_s, z_r, i).start()
-
-    loads[0].wait()
+        if i >= cut:
+            to_owner(own_sum, dst, z_s, z_r, i, cut).start()
+
+    loads[5].wait()
     psum, esum = proj.at[0], back.at[0]
     pland, eland = proj.at[1], back.at[1]
     for i in range(n_ctx + 2):
@@ -330,12 +346,14 @@
             after_core(i - 1, part, part_in, cross, pa_s, pa_r, cross_in, px_s, px_r)
         if i >= 2:
             after_x(
-                i - 2, part, part_in, cross_in, cross, px_s, px_r, pland, psum, pz_s, pz_r
+                i - 2, part, part_in, cross_in, cross, px_s, px_r, pland, psum, pz_s, pz_r, 1
             )
 
     def landed(dst, own_sum, send, recv, s):
         return to_ctx(own_sum.at[0], dst.at[s], send.at[0], recv.at[s], (z + 1) % n_ctx)
 
+    loads[6].wait()
+    loads[7].wait()
     pland[z] = psum[0]
     for i in range(1, n_ctx):
         landed(pland, psum, pz_s, pz_r, source(i)).wait_recv()
@@ -359,12 +377,12 @@
         b = h if which == 0 else x_peer
         return to_head(tok.at[s, b], tok.at[s, b], tc_s.at[s, which], tc_r.at[s, which], core_peer)
 
-    for load in loads[1:]:
+    for load in loads[8:]:
         load.wait()
     tile = 256
     expert = z * lax.axis_size("head") + h
 
-    def experts(i, s):
+    def hidden_of(s):
         tokens = tok[s, :, :, :model].reshape(4 * own, model)
         table = tok[s, :, :, model:].reshape(4 * own, LANES).astype(f32)
         at = lax.broadcasted_iota(jnp.int32, table.shape, 1)
@@ -375,15 +393,31 @@
             gate_act = jnp.dot(tokens, wg[:, columns], preferred_element_type=f32)
             up_act = jnp.dot(tokens, wu[:, columns], preferred_element_type=f32)
             acts.append((gate_act * (up_act / (1.0 + jnp.exp(-gate_act)))).astype(bf16))
-        hid = jnp.concatenate(acts, axis=1)
-
-        @pl.loop(0, model // tile)
+        return jnp.concatenate(acts, axis=1), weight
+
+    width = model // CUT
+
+    def output_of(i, hid, weight):
+        first = (i % CUT) * width
+
+        @pl.loop(0, width // tile)
         def _(t):
             columns = pl.ds(pl.multiple_of(t * tile, tile), tile)
-            value = jnp.dot(hid, wd[:, columns], preferred_element_type=f32)
+            source_columns = pl.ds(pl.multiple_of(first + t * tile, tile), tile)
+            value = jnp.dot(hid, wd[:, source_columns], preferred_element_type=f32)
             store_chunk(epart, i, columns, value.astype(bf16).astype(f32) * weight)
 
-    for i in range(n_ctx + 3):
+        swap_core(epart, epart_in, ea_s, ea_r, i).start()
+
+    def experts_core(i):
+        after_core(i, epart, epart_in, ecross, ea_s, ea_r, ecross_in, ex_s, ex_r)
+
+    def experts_x(i):
+        after_x(
+            i, epart, epart_in, ecross_in, ecross, ex_s, ex_r, eland, esum, ez_s, ez_r, CUT
+        )
+
+    for i in range(n_ctx + 2):
         if i < n_ctx:
             s = source(i)
             if i > 0:
@@ -397,27 +431,29 @@
             tok_c(s, 1).start()
             tok_c(s, 0).wait_recv()
             tok_c(s, 1).wait_recv()
-            experts(i - 1, s)
-            swap_core(epart, epart_in, ea_s, ea_r, i - 1).start()
-        if 2 <= i <= n_ctx + 1:
-            after_core(i - 2, epart, epart_in, ecross, ea_s, ea_r, ecross_in, ex_s, ex_r)
-        if i >= 3:
-            after_x(
-                i - 3, epart, epart_in, ecross_in, ecross, ex_s, ex_r, eland, esum, ez_s, ez_r
-            )
-
-    total = esum[0].astype(f32)
-    for i in range(1, n_ctx):
-        s = source(i)
-        landed(eland, esum, ez_s, ez_r, s).wait_recv()
-        total = total + eland[s].astype(f32)
-    out_ref[...] = total.astype(bf16)
-
-    for s in range(n_ctx):
-
-        @pl.when((s <= z) & (z < last))
+            hid, weight = hidden_of(s)
+        if i >= 2:
+            for c in range(CUT):
+                experts_core((i - 2) * CUT + c)
+        for c in range(CUT):
+            if 1 <= i <= n_ctx:
+                output_of((i - 1) * CUT + c, hid, weight)
+            if i >= 2:
+                experts_x((i - 2) * CUT + c)
+
+    for c in range(CUT):
+        total = esum[c].astype(f32)
+        for i in range(1, n_ctx):
+            slot = source(i) * CUT + c
+            landed(eland, esum, ez_s, ez_r, slot).wait_recv()
+            total = total + eland[slot].astype(f32)
+        out_ref[:, c * width : (c + 1) * width] = total.astype(bf16)
+
+    for step in range(1, n_ctx):
+
+        @pl.when(z + step <= last)
         def _():
-            kv_copy(s).wait_send()
+            kv_copy(z, step).wait_send()
 
     for i in range(n_ctx):
         s = source(i)
@@ -428,12 +464,14 @@
         tok_c(s, 0).wait_send()
         tok_c(s, 1).wait_send()
         swap_core(part, part_in, pa_s, pa_r, i).wait_send()
+        swap_x(cross, cross_in, px_s, px_r, i).wait_send()
+        if i > 0:
+            to_owner(psum, pland, pz_s, pz_r, i, 1).wait_send()
+    for i in range(n_ctx * CUT):
         swap_core(epart, epart_in, ea_s, ea_r, i).wait_send()
-        swap_x(cross, cross_in, px_s, px_r, i).wait_send()
         swap_x(ecross, ecross_in, ex_s, ex_r, i).wait_send()
-        if i > 0:
-            to_owner(psum, pland, pz_s, pz_r, i).wait_send()
-            to_owner(esum, eland, ez_s, ez_r, i).wait_send()
+        if i >= CUT:
+            to_owner(esum, eland, ez_s, ez_r, i, CUT).wait_send()
 
 
 def fused(query, keys, values, residual, o_weight, gain, routes, gates, w_gate, w_up, w_down):
@@ -444,16 +482,16 @@
     block = o_weight.shape[1]
     bf16 = jnp.bfloat16
     vmem = pl.BlockSpec(memory_space=pltpu.VMEM)
-    hbm = pl.BlockSpec(memory_space=pl.ANY)
+    hbm = pl.BlockSpec(memory_space=pltpu.HBM)
     dma = pltpu.SemaphoreType.DMA
 
-    def sums(columns):
+    def sums(slots, columns):
         return [
-            pltpu.VMEM((n, 2, 2, own, columns), bf16),
-            pltpu.VMEM((n, 2, own, columns), bf16),
-            pltpu.VMEM((n, own, columns), bf16),
-            pltpu.VMEM((n, own, columns), bf16),
-            pltpu.VMEM((2, n, own, columns), bf16),
+            pltpu.VMEM((slots, 2, 2, own, columns), bf16),
+            pltpu.VMEM((slots, 2, own, columns), bf16),
+            pltpu.VMEM((slots, own, columns), bf16),
+            pltpu.VMEM((slots, own, columns), bf16),
+            pltpu.VMEM((2, slots, own, columns), bf16),
         ]
 
     flops = 2 * rows * (width * model // 1 + 2 * n * rows * width) + 24 * n * rows * model * hidden // 4
@@ -463,34 +501,39 @@
             jax.ShapeDtypeStruct(residual.shape, bf16),
             jax.ShapeDtypeStruct(residual.shape, bf16),
         ),
-        in_specs=[vmem, vmem, vmem, vmem, hbm, vmem, vmem, vmem, hbm, hbm, hbm],
+        in_specs=[hbm] * 11,
         out_specs=(vmem, vmem),
         scratch_shapes=[
+            pltpu.VMEM(query.shape, bf16),
+            pltpu.VMEM(residual.shape, bf16),
+            pltpu.VMEM((1, model), jnp.float32),
+            pltpu.VMEM(routes.shape[::-1], jnp.int32),
+            pltpu.VMEM(gates.shape[::-1], jnp.float32),
             pltpu.VMEM(o_weight.shape, bf16),
             pltpu.VMEM(w_gate.shape[1:], bf16),
             pltpu.VMEM(w_up.shape[1:], bf16),
             pltpu.VMEM(w_down.shape[1:], bf16),
             pltpu.VMEM((n, 2, rows, HEAD_DIMENSION), bf16),
             pltpu.VMEM((n, PIECES, rows, width // PIECES), bf16),
-            *sums(block),
+            *sums(n, block),
             pltpu.VMEM((n, 4, own, model + LANES), bf16),
-            *sums(model),
-            dma((4,)),
+            *sums(n * CUT, model // CUT),
+            dma((11,)),
             dma((n,)), dma((n,)),
             dma((n, PIECES, 2)), dma((n, PIECES)),
             dma((n,)), dma((n,)), dma((n,)), dma((n,)), dma((n,)), dma((n,)),
             dma((n, 2)), dma((n,)), dma((n,)), dma((n,)), dma((n, 2)), dma((n, 2)),
-            dma((n,)), dma((n,)), dma((n,)), dma((n,)), dma((n,)), dma((n,)),
+            *[dma((n * CUT,))] * 6,
         ],
         compiler_params=pltpu.CompilerParams(
-            collective_id=0, has_side_effects=True, vmem_limit_bytes=48 * 1024 * 1024
+            collective_id=0, has_side_effects=True, vmem_limit_bytes=56 * 1024 * 1024
         ),
         cost_estimate=pl.CostEstimate(
             flops=flops, bytes_accessed=6 * model * hidden + 2 * width * block, transcendentals=0
         ),
         name="layer",
     )(
-        query, keys, values, residual, o_weight, gain.reshape(1, -1), routes, gates,
+        query, keys, values, residual, o_weight, gain.reshape(1, -1), routes.T, gates.T,
         w_gate, w_up, w_down,
     )
 

time: 97 us -> 88 us (0.907)
  local copies, waits for them, and re-layouts: 10 us -> 3.14 us
  Pallas kernels: 85.8 us -> 84.1 us
    unnamed x18 -> x2, local copies, waits for them, and re-layouts: 10 us -> 3.14 us
    pallas_call x1, Pallas kernels: 85.8 us -> 84.1 us  [fused(): pl.pallas_call(lambda *refs: layer_kernel(n, *refs), out_shape=(jax.Shape...]
where the time goes in v2:
time: 88 us; the launch traced here: 87.8 us
  Pallas kernels  84.1 us (96%)
  local copies, waits for them, and re-layouts  3.14 us (4%)
    pallas_call x1, Pallas kernels, fused(): pl.pallas_call(lambda *refs: layer_kernel(n, *refs), out_shape=(jax.Shape...  84.1 us
    unnamed x2, local copies, waits for them, and re-layouts  3.14 us

profile of v2, /device:TPU:0, one launch (start us, length us, event | category | flops | bytes accessed | tf_op | source)
XLA Modules:
  0.0 87.8 jit_solution(16767102645856800671)
XLA Ops:
  0.6 84.1 %layer.1 = (bf16[32,2048]{1,0:T(8,128)(2,1)}, bf16[32,2048]{1,0:T(8,128)(2,1)}) custom-call(bf16[128,1024]{1,0:T(8,128)(2,1)} %refs_0_.1, bf16[128,128]{1,0:T(8,128)(2,1)} %refs_1_.1, bf16[128,128]{1,0:T(8,128)(2,1)} %refs_2_.1, bf16[32,2048]{1,0:T(8,128)(2,1)} %refs_3_.1, bf16[1024,512]{1,0:T(8,128)(2,1)} %refs_4_.1, f32[1,2048]{1,0:T(1,128)} %bitcast.3, ...), custom_call_target="tpu_custom_call" | custom-call | flops 5637144576 | bytes 10485760 | tf_op jit(solution)/shard_map/layer/pallas_call | solution.py:498
  84.7 1.6 %copy.15 = bf16[32,2048]{1,0:T(8,128)(2,1)} copy(bf16[32,2048]{1,0:T(8,128)(2,1)} %get-tuple-element.4) | data formatting | bytes 262144
  86.3 1.6 %copy.16 = bf16[32,2048]{1,0:T(8,128)(2,1)} copy(bf16[32,2048]{1,0:T(8,128)(2,1)} %get-tuple-element.5) | data formatting | bytes 262144

commit v3 on v2

--- a/solution.py
+++ b/solution.py
@@ -135,10 +135,10 @@
     q_hbm, k_hbm, v_hbm, res_hbm, wo_hbm, gain_hbm, routes_hbm, gates_hbm, wg_hbm, wu_hbm, wd_hbm,
     mixed_ref, out_ref,
     q_ref, res_ref, gain_ref, routes_ref, gates_ref, wo, wg, wu, wd,
-    kv, att, part, part_in, cross, cross_in, proj,
+    kv, att, part, part_in, proj,
     tok, epart, epart_in, ecross, ecross_in, back,
     local_sem,
-    kv_s, kv_r, att_s, att_r, pa_s, pa_r, px_s, px_r, pz_s, pz_r,
+    kv_s, kv_r, att_s, att_r, pa_s, pa_r, pz_s, pz_r,
     tz_s, tz_r, tx_s, tx_r, tc_s, tc_r, ea_s, ea_r, ex_s, ex_r, ez_s, ez_r,
 ):
     f32, bf16 = jnp.float32, jnp.bfloat16
@@ -177,8 +177,11 @@
         load.start()
 
     barrier = pltpu.get_barrier_semaphore()
-    for peer in (core_peer, x_peer):
-        pl.semaphore_signal(barrier, inc=1, device_id={"head": peer}, device_id_type=MESH)
+    n_head = lax.axis_size("head")
+    for step in range(1, n_head):
+        pl.semaphore_signal(
+            barrier, inc=1, device_id={"head": (h + step) % n_head}, device_id_type=MESH
+        )
     for step in range(1, n_ctx):
         pl.semaphore_signal(
             barrier, inc=1, device_id={"ctx": (z + step) % n_ctx}, device_id_type=MESH
@@ -205,7 +208,7 @@
     high = table.astype(bf16).astype(f32)
     tok[z, h, :, model:] = jnp.where(lane < half, high, table - high).astype(bf16)
 
-    pl.semaphore_wait(barrier, n_ctx + 1)
+    pl.semaphore_wait(barrier, n_ctx + n_head - 2)
 
     def to_ctx(src, dst, send, recv, target):
         return pltpu.make_async_remote_copy(
@@ -283,7 +286,7 @@
             )
             scores = jnp.where(visible, scores * scale, -1e30)
             top = jnp.max(scores, axis=-1, keepdims=True)
-            weights = jnp.where(visible, jnp.exp(scores - top), 0.0)
+            weights = jnp.exp(scores - top)
             total = jnp.sum(weights, axis=-1, keepdims=True)
             summed = jnp.dot(weights.astype(bf16), values_all, preferred_element_type=f32)
             att[z, p, :, j * size : (j + 1) * size] = (summed / total).astype(bf16)
@@ -298,6 +301,13 @@
     def to_owner(buf, dst, send, recv, i, cut):
         slot = z * cut + i % cut
         return to_ctx(buf.at[i], dst.at[slot], send.at[i], recv.at[slot], source(i // cut))
+
+    def to_head_owner(i, step):
+        peer = (h + step) % n_head
+        return to_head(
+            part.at[i, peer], part_in.at[i, step - 1],
+            pa_s.at[i, step - 1], pa_r.at[i, step - 1], peer,
+        )
 
     def store_chunk(buf, i, columns, value):
         parts = value.astype(bf16).reshape(2, 2, own, value.shape[-1])
@@ -326,7 +336,7 @@
     loads[5].wait()
     psum, esum = proj.at[0], back.at[0]
     pland, eland = proj.at[1], back.at[1]
-    for i in range(n_ctx + 2):
+    for i in range(n_ctx + 1):
         if i < n_ctx:
             s = source(i)
             value = None
@@ -340,14 +350,17 @@
                     preferred_element_type=f32,
                 )
                 value = term if value is None else value + term
-            store_chunk(part, i, slice(None), value)
-            swap_core(part, part_in, pa_s, pa_r, i).start()
-        if 1 <= i <= n_ctx:
-            after_core(i - 1, part, part_in, cross, pa_s, pa_r, cross_in, px_s, px_r)
-        if i >= 2:
-            after_x(
-                i - 2, part, part_in, cross_in, cross, px_s, px_r, pland, psum, pz_s, pz_r, 1
-            )
+            part[i] = value.astype(bf16).reshape(part.shape[1:])
+            for step in range(1, n_head):
+                to_head_owner(i, step).start()
+        if i >= 1:
+            value = part[i - 1, h].astype(f32)
+            for step in range(1, n_head):
+                to_head_owner(i - 1, step).wait_recv()
+                value = value + part_in[i - 1, step - 1].astype(f32)
+            psum[i - 1] = value.astype(bf16)
+            if i >= 2:
+                to_owner(psum, pland, pz_s, pz_r, i - 1, 1).start()
 
     def landed(dst, own_sum, send, recv, s):
         return to_ctx(own_sum.at[0], dst.at[s], send.at[0], recv.at[s], (z + 1) % n_ctx)
@@ -396,15 +409,18 @@
         return jnp.concatenate(acts, axis=1), weight
 
     width = model // CUT
+    wide = min(512, width)
 
     def output_of(i, hid, weight):
         first = (i % CUT) * width
 
-        @pl.loop(0, width // tile)
-        def _(t):
-            columns = pl.ds(pl.multiple_of(t * tile, tile), tile)
-            source_columns = pl.ds(pl.multiple_of(first + t * tile, tile), tile)
-            value = jnp.dot(hid, wd[:, source_columns], preferred_element_type=f32)
+        for t in range(width // wide):
+            columns = slice(t * wide, (t + 1) * wide)
+            value = jnp.dot(
+                hid,
+                wd[:, first + t * wide : first + (t + 1) * wide],
+                preferred_element_type=f32,
+            )
             store_chunk(epart, i, columns, value.astype(bf16).astype(f32) * weight)
 
         swap_core(epart, epart_in, ea_s, ea_r, i).start()
@@ -463,8 +479,8 @@
         tok_x(s).wait_send()
         tok_c(s, 0).wait_send()
         tok_c(s, 1).wait_send()
-        swap_core(part, part_in, pa_s, pa_r, i).wait_send()
-        swap_x(cross, cross_in, px_s, px_r, i).wait_send()
+        for step in range(1, n_head):
+            to_head_owner(i, step).wait_send()
         if i > 0:
             to_owner(psum, pland, pz_s, pz_r, i, 1).wait_send()
     for i in range(n_ctx * CUT):
@@ -475,7 +491,7 @@
 
 
 def fused(query, keys, values, residual, o_weight, gain, routes, gates, w_gate, w_up, w_down):
-    n = lax.axis_size("ctx")
+    n, heads = lax.axis_size("ctx"), lax.axis_size("head")
     rows, width = query.shape
     own, model = residual.shape
     hidden = w_gate.shape[2]
@@ -515,18 +531,20 @@
             pltpu.VMEM(w_down.shape[1:], bf16),
             pltpu.VMEM((n, 2, rows, HEAD_DIMENSION), bf16),
             pltpu.VMEM((n, PIECES, rows, width // PIECES), bf16),
-            *sums(n, block),
+            pltpu.VMEM((n, heads, own, block), bf16),
+            pltpu.VMEM((n, heads - 1, own, block), bf16),
+            pltpu.VMEM((2, n, own, block), bf16),
             pltpu.VMEM((n, 4, own, model + LANES), bf16),
             *sums(n * CUT, model // CUT),
             dma((11,)),
             dma((n,)), dma((n,)),
             dma((n, PIECES, 2)), dma((n, PIECES)),
-            dma((n,)), dma((n,)), dma((n,)), dma((n,)), dma((n,)), dma((n,)),
+            dma((n, heads - 1)), dma((n, heads - 1)), dma((n,)), dma((n,)),
             dma((n, 2)), dma((n,)), dma((n,)), dma((n,)), dma((n, 2)), dma((n, 2)),
             *[dma((n * CUT,))] * 6,
         ],
         compiler_params=pltpu.CompilerParams(
-            collective_id=0, has_side_effects=True, vmem_limit_bytes=56 * 1024 * 1024
+            collective_id=0, has_side_effects=True, vmem_limit_bytes=44 * 1024 * 1024
         ),
         cost_estimate=pl.CostEstimate(
             flops=flops, bytes_accessed=6 * model * hidden + 2 * width * block, transcendentals=0

time: 88 us -> 96.2 us (1.093)
  local copies, waits for them, and re-layouts: 3.14 us -> 11.7 us
    unnamed x2 -> x22, local copies, waits for them, and re-layouts: 3.14 us -> 11.7 us
where the time goes in v3:
time: 96.2 us; the launch traced here: 95.6 us
  Pallas kernels  83.2 us (86%)
  local copies, waits for them, and re-layouts  11.7 us (12%)
    pallas_call x1, Pallas kernels, fused(): pl.pallas_call(lambda *refs: layer_kernel(n, *refs), out_shape=(jax.Shape...  83.2 us
    unnamed x22, local copies, waits for them, and re-layouts  11.7 us

profile of v3, /device:TPU:0, one launch (start us, length us, event | category | flops | bytes accessed | tf_op | source)
XLA Modules:
  0.0 95.6 jit_solution(578804099289796135)
XLA Ops:
  0.6 0.0 copy-start
  0.6 1.9 %copy-done = bf16[1,2048,768]{2,1,0:T(8,128)(2,1)S(1)} copy-done((bf16[1,2048,768]{2,1,0:T(8,128)(2,1)S(1)}, bf16[1,2048,768]{2,1,0:T(8,128)(2,1)}, u32[]{:S(2)}) %copy-start) | copy-done | bytes 3145752
  2.5 0.0 copy-start.1
  2.5 1.9 %copy-done.1 = bf16[1,2048,768]{2,1,0:T(8,128)(2,1)S(1)} copy-done((bf16[1,2048,768]{2,1,0:T(8,128)(2,1)S(1)}, bf16[1,2048,768]{2,1,0:T(8,128)(2,1)}, u32[]{:S(2)}) %copy-start.1) | copy-done | bytes 3145752
  4.4 0.0 copy-start.2
  4.4 1.2 %copy-done.2 = bf16[1024,512]{1,0:T(8,128)(2,1)S(1)} copy-done((bf16[1024,512]{1,0:T(8,128)(2,1)S(1)}, bf16[1024,512]{1,0:T(8,128)(2,1)}, u32[]{:S(2)}) %copy-start.2) | copy-done | bytes 1048600
  5.6 0.0 copy-start.3
  5.6 0.9 copy-done.3
  6.6 0.0 copy-start.4
  6.6 0.9 copy-done.4
  7.5 0.0 copy-start.5
  7.5 0.8 copy-done.5
  8.3 0.0 copy-start.6
  8.3 0.8 copy-done.6
  9.0 0.0 copy-start.7
  9.0 0.7 copy-done.7
  9.7 0.0 copy-start.8
  9.7 0.7 copy-done.8
  10.4 0.0 copy-start.9
  10.4 0.7 copy-done.9
  11.1 83.2 %layer.1 = (bf16[32,2048]{1,0:T(8,128)(2,1)S(1)}, bf16[32,2048]{1,0:T(8,128)(2,1)S(1)}) custom-call(bf16[128,1024]{1,0:T(8,128)(2,1)S(1)} %copy-done.3, bf16[128,128]{1,0:T(8,128)(2,1)S(1)} %copy-done.5, bf16[128,128]{1,0:T(8,128)(2,1)S(1)} %copy-done.6, bf16[32,2048]{1,0:T(8,128)(2,1)S(1)} %copy-done.4, bf16[1024,512]{1,0:T(8,128)(2,1)S(1)} %copy-done.2, ...), custom_call_target="tpu_custom_call" | custom-call | flops 5637144576 | bytes 10485760 | tf_op jit(solution)/shard_map/layer/pallas_call | solution.py:514
  94.3 0.7 copy.15
  95.0 0.7 copy.16
Async XLA Ops:
  0.6 1.9 %copy-start = (bf16[1,2048,768]{2,1,0:T(8,128)(2,1)S(1)}, bf16[1,2048,768]{2,1,0:T(8,128)(2,1)}, u32[]{:S(2)}) copy-start(bf16[1,2048,768]{2,1,0:T(8,128)(2,1)} %refs_8_.1) | copy-start | bytes 9437188
  2.5 1.9 %copy-start.1 = (bf16[1,2048,768]{2,1,0:T(8,128)(2,1)S(1)}, bf16[1,2048,768]{2,1,0:T(8,128)(2,1)}, u32[]{:S(2)}) copy-start(bf16[1,2048,768]{2,1,0:T(8,128)(2,1)} %refs_9_.1) | copy-start | bytes 9437188
  4.4 1.2 %copy-start.2 = (bf16[1024,512]{1,0:T(8,128)(2,1)S(1)}, bf16[1024,512]{1,0:T(8,128)(2,1)}, u32[]{:S(2)}) copy-start(bf16[1024,512]{1,0:T(8,128)(2,1)} %refs_4_.1) | copy-start | bytes 3145732
  5.6 0.9 copy-start.3
  6.6 0.9 copy-start.4
  7.5 0.8 copy-start.5
  8.3 0.8 copy-start.6
  9.0 0.7 copy-start.7
  9.7 0.7 copy-start.8
  10.4 0.7 copy-start.9

commit v4 on v3

--- a/solution.py
+++ b/solution.py
@@ -433,29 +433,47 @@
             i, epart, epart_in, ecross_in, ecross, ex_s, ex_r, eland, esum, ez_s, ez_r, CUT
         )
 
-    for i in range(n_ctx + 2):
-        if i < n_ctx:
-            s = source(i)
-            if i > 0:
-                tok_z(s, True).wait_recv()
-            chain_each(i, s, lambda right, s=s: tok_z(s, right).start())
-            tok_x(s).start()
-            tok_c(s, 0).start()
-        if 1 <= i <= n_ctx:
-            s = source(i - 1)
-            tok_x(s).wait_recv()
-            tok_c(s, 1).start()
-            tok_c(s, 0).wait_recv()
-            tok_c(s, 1).wait_recv()
-            hid, weight = hidden_of(s)
-        if i >= 2:
-            for c in range(CUT):
-                experts_core((i - 2) * CUT + c)
+    def spread(i):
+        s = source(i)
+        if i > 0:
+            tok_z(s, True).wait_recv()
+        chain_each(i, s, lambda right, s=s: tok_z(s, right).start())
+        tok_x(s).start()
+        tok_c(s, 0).start()
+
+    def crossed_tokens(i):
+        s = source(i)
+        tok_x(s).wait_recv()
+        tok_c(s, 1).start()
+
+    order = [*range(1, n_ctx), 0]
+    spread(0)
+    spread(1)
+    crossed_tokens(order[0])
+    for i in range(2, min(3, n_ctx)):
+        spread(i)
+    before = None
+    for turn, i in enumerate(order):
+        s = source(i)
+        tok_c(s, 0).wait_recv()
+        tok_c(s, 1).wait_recv()
+        hid, weight = hidden_of(s)
+        if turn + 3 < n_ctx:
+            spread(turn + 3)
+        if turn + 1 < n_ctx:
+            crossed_tokens(order[turn + 1])
         for c in range(CUT):
-            if 1 <= i <= n_ctx:
-                output_of((i - 1) * CUT + c, hid, weight)
-            if i >= 2:
-                experts_x((i - 2) * CUT + c)
+            if before is not None:
+                experts_core(before * CUT + c)
+        for c in range(CUT):
+            output_of(i * CUT + c, hid, weight)
+            if before is not None:
+                experts_x(before * CUT + c)
+        before = i
+    for c in range(CUT):
+        experts_core(before * CUT + c)
+    for c in range(CUT):
+        experts_x(before * CUT + c)
 
     for c in range(CUT):
         total = esum[c].astype(f32)
@@ -544,7 +562,7 @@
             *[dma((n * CUT,))] * 6,
         ],
         compiler_params=pltpu.CompilerParams(
-            collective_id=0, has_side_effects=True, vmem_limit_bytes=44 * 1024 * 1024
+            collective_id=0, has_side_effects=True, vmem_limit_bytes=56 * 1024 * 1024
         ),
         cost_estimate=pl.CostEstimate(
             flops=flops, bytes_accessed=6 * model * hidden + 2 * width * block, transcendentals=0
@@ -564,7 +582,7 @@
     return (
         capacity == own
         and mesh.shape["head"] == 4
-        and mesh.shape["ctx"] <= 8
+        and 2 <= mesh.shape["ctx"] <= 8
         and args[8].shape[0] == devices
         and devices <= LANES // 2
         and own % 16 == 0

time: 96.2 us -> 86.3 us (0.90)
  local copies, waits for them, and re-layouts: 11.7 us -> 3.14 us
    unnamed x22 -> x2, local copies, waits for them, and re-layouts: 11.7 us -> 3.14 us
where the time goes in v4:
time: 86.3 us; the launch traced here: 86.2 us
  Pallas kernels  82.4 us (95%)
  local copies, waits for them, and re-layouts  3.14 us (4%)
    pallas_call x1, Pallas kernels, fused(): pl.pallas_call(lambda *refs: layer_kernel(n, *refs), out_shape=(jax.Shape...  82.4 us
    unnamed x2, local copies, waits for them, and re-layouts  3.14 us

profile of v4, /device:TPU:0, one launch (start us, length us, event | category | flops | bytes accessed | tf_op | source)
XLA Modules:
  0.0 86.2 jit_solution(6300255557632665274)
XLA Ops:
  0.6 82.4 %layer.1 = (bf16[32,2048]{1,0:T(8,128)(2,1)}, bf16[32,2048]{1,0:T(8,128)(2,1)}) custom-call(bf16[128,1024]{1,0:T(8,128)(2,1)} %refs_0_.1, bf16[128,128]{1,0:T(8,128)(2,1)} %refs_1_.1, bf16[128,128]{1,0:T(8,128)(2,1)} %refs_2_.1, bf16[32,2048]{1,0:T(8,128)(2,1)} %refs_3_.1, bf16[1024,512]{1,0:T(8,128)(2,1)} %refs_4_.1, f32[1,2048]{1,0:T(1,128)} %bitcast.3, ...), custom_call_target="tpu_custom_call" | custom-call | flops 5637144576 | bytes 10485760 | tf_op jit(solution)/shard_map/layer/pallas_call | solution.py:532
  83.0 1.6 %copy.15 = bf16[32,2048]{1,0:T(8,128)(2,1)} copy(bf16[32,2048]{1,0:T(8,128)(2,1)} %get-tuple-element.4) | data formatting | bytes 262144
  84.6 1.6 %copy.16 = bf16[32,2048]{1,0:T(8,128)(2,1)} copy(bf16[32,2048]{1,0:T(8,128)(2,1)} %get-tuple-element.5) | data formatting | bytes 262144
